TPU v7x, 256 devices: a whole 4x4x8 slice. The times are simulated.
256 devices in a mesh: subtree: 16 (over z, core), front: 16 (over x, y).
Axes of the slice: x: 4, y: 4, z: 8, core: 2. Of those that a mesh axis runs over, the one named last changes fastest.
Arguments:
- leaf_rhs: float32 [16, 2048, 256], P('subtree', 'front'), may hold values from -6 to 6
- mid_rhs: float32 [4, 4096, 256], P(None, 'front'), may hold values from -6 to 6
- root_rhs: float32 [10240, 256], P('front'), may hold values from -6 to 6
- leaf_lower: float32 [16, 2048, 2048], P('subtree', None, 'front'), may hold values from -0.125 to 0.125
- leaf_below: float32 [16, 2048, 2048], P('subtree', None, 'front'), may hold values from -0.125 to 0.125
- leaf_right: float32 [16, 2048, 2048], P('subtree', None, 'front'), may hold values from -0.125 to 0.125
- leaf_upper: float32 [16, 2048, 2048], P('subtree', None, 'front'), may hold values from -0.125 to 0.125
- mid_lower: float32 [4, 4096, 4096], P(None, 'subtree', 'front'), may hold values from -0.09375 to 0.09375
- mid_below: float32 [4, 4096, 4096], P(None, 'front', 'subtree'), may hold values from -0.09375 to 0.09375
- mid_right: float32 [4, 4096, 4096], P(None, 'subtree', 'front'), may hold values from -0.09375 to 0.09375
- mid_upper: float32 [4, 4096, 4096], P(None, 'front', 'subtree'), may hold values from -0.09375 to 0.09375
- root_lower: float32 [10240, 10240], P('subtree', 'front'), may hold values from -0.0625 to 0.0625
- root_upper: float32 [10240, 10240], P('front', 'subtree'), may hold values from -0.0625 to 0.0625
- leaf_parent: int32 [16], replicated, may hold values from 0 to 3, as said below
- leaf_sizes: int32 [16], replicated, may hold values from 1024 to 2048, as said below
- leaf_map: int32 [16, 16], replicated, may hold values from 0 to 63, as said below
- mid_map: int32 [4, 32], replicated, may hold values from 0 to 79, as said below
Outputs:
- leaf_sol: float32 [16, 2048, 256], P('subtree', 'front')
- mid_sol: float32 [4, 4096, 256], P(None, 'front')
- root_sol: float32 [10240, 256], P('front')
Inputs may be any that keep to these rules, and one draw needn't show every extreme that they name: `leaf_parent`: every level-1 front is the parent of at least one lowest-level front. `leaf_sizes`: a multiple of 128; some front has all 2048 rows live. `leaf_map`: a front's blocks go to distinct parent blocks; update block b of a lowest-level front, with c = b, goes to c * 2 + i or to that plus 4096 / 128, for some i with 0 <= i < 2. `mid_map`: a front's blocks go to distinct root blocks; update block b of a level-1 front, with c = b // 2, goes to c * 5 + i for some i with 0 <= i < 5.
All inputs are finite; a program needn't handle non-finite values.
Results may differ from a plain program's by a relative error of at most 0.00013.
Values sent between devices are 32-bit elements; how exact they have to be, the bound alone decides.
A program may use at most 64 MiB of HBM per device.

v0:
```python
import jax
import jax.numpy as jnp
from jax import lax
from jax.sharding import PartitionSpec as P

MID_PIV = 4096
BLOCK = 128


def leaf_product(matrix, vector):
    return lax.psum_scatter(
        jnp.dot(
            matrix, vector, preferred_element_type=jnp.float32, precision=lax.Precision.HIGHEST
        ),
        "front",
        scatter_dimension=0,
        tiled=True,
    )


def across_front(partial_value):
    return lax.psum(partial_value, "front")


def across_subtree(partial_value):
    return lax.psum(partial_value, "subtree")


def batched(matrix, vector):
    return jnp.einsum(
        "fab,fbr->far",
        matrix,
        vector,
        preferred_element_type=jnp.float32,
        precision=lax.Precision.HIGHEST,
    )


def leaf_select(parents, blocks, fronts, column, width):
    front_ids = jnp.arange(fronts, dtype=jnp.int32)[:, None, None, None, None]
    halves = jnp.arange(2, dtype=jnp.int32)[None, :, None, None, None]
    slots = jnp.arange(width, dtype=jnp.int32)[None, None, :, None, None]
    target = halves * (MID_PIV // BLOCK) + column * width + slots
    match_parent = parents[None, None, None, :, None] == front_ids
    match_block = blocks[None, None, None, :, :] == target
    return (match_parent & match_block).astype(jnp.float32)


def on_device(
    leaf_rhs,
    mid_rhs,
    root_rhs,
    leaf_lower,
    leaf_below,
    leaf_right,
    leaf_upper,
    mid_lower,
    mid_below,
    mid_right,
    mid_upper,
    root_lower,
    root_upper,
    leaf_parent,
    leaf_sizes,
    leaf_map,
    mid_map,
):
    group = lax.axis_index("subtree")
    column = lax.axis_index("front")
    local_rows = leaf_rhs.shape[1]
    scenarios = leaf_rhs.shape[2]
    leaf_width = local_rows // BLOCK
    fronts = mid_rhs.shape[0]
    mid_width = mid_rhs.shape[1] // BLOCK
    root_width = root_rhs.shape[0] // BLOCK
    own_size = lax.dynamic_slice_in_dim(leaf_sizes, group, 1)
    positions = column * local_rows + jnp.arange(local_rows, dtype=jnp.int32)
    live = (positions < own_size[0]).astype(jnp.float32)[:, None]
    leaf_fwd = live * leaf_product(leaf_lower[0], live * leaf_rhs[0])
    leaf_contrib = -leaf_product(leaf_below[0], leaf_fwd)
    own_parent = lax.dynamic_slice_in_dim(leaf_parent, group, 1)
    own_blocks = lax.dynamic_slice(leaf_map, (group, column * leaf_width), (1, leaf_width))
    own_select = leaf_select(own_parent, own_blocks, fronts, column, mid_width)
    placed = jnp.einsum(
        "phqgk,gkbr->phqbr",
        own_select,
        leaf_contrib.reshape(1, leaf_width, BLOCK, scenarios),
        preferred_element_type=jnp.float32,
        precision=lax.Precision.HIGHEST,
    )
    assembled = lax.psum(placed, "subtree")
    mid_pivot = mid_rhs + assembled[:, 0].reshape(fronts, mid_width * BLOCK, scenarios)
    mid_update = assembled[:, 1].reshape(fronts, mid_width * BLOCK, scenarios)
    mid_fwd = across_front(batched(mid_lower, mid_pivot))
    mid_contrib = mid_update - across_subtree(batched(mid_below, mid_fwd))
    column_map = lax.dynamic_slice_in_dim(mid_map, column * mid_width, mid_width, 1)
    slots = jnp.arange(root_width, dtype=jnp.int32)[:, None, None]
    root_select = (column_map[None, :, :] == column * root_width + slots).astype(jnp.float32)
    root_added = jnp.einsum(
        "qpk,pkbr->qbr",
        root_select,
        mid_contrib.reshape(fronts, mid_width, BLOCK, scenarios),
        preferred_element_type=jnp.float32,
        precision=lax.Precision.HIGHEST,
    )
    root_start = root_rhs + root_added.reshape(root_width * BLOCK, scenarios)
    root_fwd = across_front(
        jnp.dot(
            root_lower,
            root_start,
            preferred_element_type=jnp.float32,
            precision=lax.Precision.HIGHEST,
        )
    )
    root_sol = across_subtree(
        jnp.dot(
            root_upper,
            root_fwd,
            preferred_element_type=jnp.float32,
            precision=lax.Precision.HIGHEST,
        )
    )
    mid_ext = jnp.einsum(
        "qpk,qbr->pkbr",
        root_select,
        root_sol.reshape(root_width, BLOCK, scenarios),
        preferred_element_type=jnp.float32,
        precision=lax.Precision.HIGHEST,
    )
    mid_ext = mid_ext.reshape(fronts, mid_width * BLOCK, scenarios)
    mid_back = mid_fwd - across_front(batched(mid_right, mid_ext))
    mid_sol = across_subtree(batched(mid_upper, mid_back))
    whole_column = jnp.stack(
        [
            mid_sol.reshape(fronts, mid_width, BLOCK, scenarios),
            mid_ext.reshape(fronts, mid_width, BLOCK, scenarios),
        ],
        axis=1,
    )
    leaf_ext = jnp.einsum(
        "phqgk,phqbr->gkbr",
        own_select,
        whole_column,
        preferred_element_type=jnp.float32,
        precision=lax.Precision.HIGHEST,
    )
    leaf_ext = leaf_ext.reshape(local_rows, scenarios)
    leaf_back = live * (leaf_fwd - leaf_product(leaf_right[0], leaf_ext))
    leaf_sol = live * leaf_product(leaf_upper[0], leaf_back)
    return (leaf_sol[None], mid_sol, root_sol)


def solution(mesh):
    return jax.shard_map(
        on_device,
        mesh=mesh,
        in_specs=(
            P("subtree", "front", None),
            P(None, "front", None),
            P("front", None),
            P("subtree", None, "front"),
            P("subtree", None, "front"),
            P("subtree", None, "front"),
            P("subtree", None, "front"),
            P(None, "subtree", "front"),
            P(None, "front", "subtree"),
            P(None, "subtree", "front"),
            P(None, "front", "subtree"),
            P("subtree", "front"),
            P("front", "subtree"),
            P(),
            P(),
            P(),
            P(),
        ),
        out_specs=(P("subtree", "front", None), P(None, "front", None), P("front", None)),
        check_vma=False,
    )
```

profile of v0, /device:TPU:2, one launch (start us, length us, event | category | flops | bytes accessed | tf_op | source)
XLA Modules:
  0.0 1138.0 jit_solution(16406673593648524195)
XLA Ops:
  7.2 0.0 reduce-scatter.5.cloned.1.call-start
  7.2 1.4 dynamic_slice.12
  8.6 0.6 compare_convert_fusion
  9.3 4.6 convolution_bitcast_fusion.3
  13.9 0.0 reduce-scatter.7.cloned.1.call-start
  14.0 82.1 %reduce-scatter.5.cloned.1.call-done = f32[128,256]{0,1:T(8,128)} async-done(((f32[2048,256]{0,1:T(8,128)}), f32[128,256]{0,1:T(8,128)}) %reduce-scatter.5.cloned.1.call-update) | async-done | bytes 131088 | tf_op jit(solution)/shard_map/reduce_scatter | solution.py:11
  96.0 4.0 convolution_bitcast_fusion.2
  100.1 0.0 reduce-scatter.7.cloned.1.call-update
  100.1 0.0 all-reduce.8.cloned.1.call-start
  100.1 0.6 dynamic_slice.13
  100.7 1.3 dynamic_slice.14
  102.0 0.6 iota_compare_fusion
  102.7 0.7 add_compare_fusion
  103.4 0.1 and_convert_fusion
  103.5 75.5 %reduce-scatter.7.cloned.1.call-done = f32[128,256]{0,1:T(8,128)} async-done(((f32[2048,256]{0,1:T(8,128)}), f32[128,256]{0,1:T(8,128)}) %reduce-scatter.7.cloned.1.call-update) | async-done | bytes 131088 | tf_op jit(solution)/shard_map/reduce_scatter | solution.py:11
  179.0 0.9 neg.3
  179.9 1.9 broadcast_multiply_fusion
  181.8 0.0 all-reduce.8.cloned.1.call-update
  181.8 0.0 all-reduce.10.cloned.1.call-start
  181.9 114.8 %all-reduce.8.cloned.1.call-done = f32[4,2,2,128,256]{3,2,4,0,1:T(2,128)} async-done(((f32[4,2,2,128,256]{3,2,4,0,1:T(2,128)}), f32[4,2,2,128,256]{3,2,4,0,1:T(2,128)}) %all-reduce.8.cloned.1.call-update) | async-done | bytes 2097168 | tf_op jit(solution)/shard_map/psum | solution.py:91
  296.7 2.7 fusion.27
  299.4 1.3 copy.29
  300.7 4.8 convolution_bitcast_fusion.8
  305.5 0.0 all-reduce.12.cloned.1.call-start
  305.6 96.9 %all-reduce.10.cloned.1.call-done = f32[4,256,256]{1,2,0:T(8,128)} async-done(((f32[4,256,256]{1,2,0:T(8,128)}), f32[4,256,256]{1,2,0:T(8,128)}) %all-reduce.10.cloned.1.call-update) | async-done | bytes 1048592 | tf_op jit(solution)/shard_map/psum | solution.py:22
  402.5 3.3 convolution_bitcast_fusion.7
  405.8 0.0 all-reduce.12.cloned.1.call-update
  405.9 0.2 all-reduce.14.cloned.1.call-start
  406.1 0.1 constant_dynamic-slice_fusion
  406.2 0.1 copy.31
  406.3 2.1 reshape_squeeze.7
  408.4 108.8 %all-reduce.12.cloned.1.call-done = f32[4,256,256]{1,2,0:T(8,128)} async-done(((f32[4,256,256]{1,2,0:T(8,128)}), f32[4,256,256]{1,2,0:T(8,128)}) %all-reduce.12.cloned.1.call-update) | async-done | bytes 1048592 | tf_op jit(solution)/shard_map/psum | solution.py:26
  517.2 2.3 sub.9
  519.5 1.7 reshape.97
  521.2 1.3 copy.32
  522.5 2.2 convolution_bitcast_fusion.4
  524.7 0.2 copy.33
  525.0 0.1 bitcast_add_fusion
  525.1 4.1 convolution_bitcast_fusion.10
  529.2 0.0 all-reduce.16.cloned.1.call-start
  529.3 95.2 %all-reduce.14.cloned.1.call-done = f32[640,256]{0,1:T(8,128)} async-done(((f32[640,256]{0,1:T(8,128)}), f32[640,256]{0,1:T(8,128)}) %all-reduce.14.cloned.1.call-update) | async-done | bytes 655376 | tf_op jit(solution)/shard_map/psum | solution.py:22
  624.5 4.0 convolution_bitcast_fusion.9
  628.5 0.0 all-reduce.18.cloned.1.call-start
  628.6 110.2 %all-reduce.16.cloned.1.call-done = f32[640,256]{0,1:T(8,128)} async-done(((f32[640,256]{0,1:T(8,128)}), f32[640,256]{0,1:T(8,128)}) %all-reduce.16.cloned.1.call-update) | async-done | bytes 655376 | tf_op jit(solution)/shard_map/psum | solution.py:26
  738.8 1.3 copy.34
  740.1 1.2 fusion.4
  741.3 4.1 convolution_bitcast_fusion.6
  745.4 0.0 all-reduce.18.cloned.1.call-update
  745.5 0.3 all-reduce.20.cloned.1.call-start
  745.7 96.9 %all-reduce.18.cloned.1.call-done = f32[4,256,256]{1,2,0:T(8,128)} async-done(((f32[4,256,256]{1,2,0:T(8,128)}), f32[4,256,256]{1,2,0:T(8,128)}) %all-reduce.18.cloned.1.call-update) | async-done | bytes 1048592 | tf_op jit(solution)/shard_map/psum | solution.py:22
  842.6 4.0 convolution_bitcast_fusion.5
  846.7 0.0 reduce-scatter.9.cloned.1.call-start
  846.7 0.1 copy.44
  846.9 111.0 %all-reduce.20.cloned.1.call-done = f32[4,256,256]{1,2,0:T(8,128)} async-done(((f32[4,256,256]{1,2,0:T(8,128)}), f32[4,256,256]{1,2,0:T(8,128)}) %all-reduce.20.cloned.1.call-update) | async-done | bytes 1048592 | tf_op jit(solution)/shard_map/psum | solution.py:26
  957.9 2.5 copy.36
  960.4 3.4 fusion
  963.8 3.2 convolution_bitcast_fusion.1
  967.1 0.0 reduce-scatter.11.cloned.1.call-start
  967.1 79.3 %reduce-scatter.9.cloned.1.call-done = f32[128,256]{0,1:T(8,128)} async-done(((f32[2048,256]{0,1:T(8,128)}), f32[128,256]{0,1:T(8,128)}) %reduce-scatter.9.cloned.1.call-update) | async-done | bytes 131088 | tf_op jit(solution)/shard_map/reduce_scatter | solution.py:11
  1046.4 4.4 convolution_bitcast_fusion
  1050.9 1.3 copy.38
  1052.2 77.6 %reduce-scatter.11.cloned.1.call-done = f32[128,256]{0,1:T(8,128)} async-done(((f32[2048,256]{0,1:T(8,128)}), f32[128,256]{0,1:T(8,128)}) %reduce-scatter.11.cloned.1.call-update) | async-done | bytes 131088 | tf_op jit(solution)/shard_map/reduce_scatter | solution.py:11
  1129.8 0.9 multiply_bitcast_fusion
  1130.7 0.8 copy.37
  (31 shorter events, 0.2 us)
Async XLA Ops:
  7.2 517.9 %copy-start = (f32[640,640]{1,0:T(8,128)S(1)}, f32[640,640]{1,0:T(8,128)}, u32[]{:S(2)}) copy-start(f32[640,640]{1,0:T(8,128)} %param.28) | copy-start | bytes 4915204
  7.2 88.8 %reduce-scatter.5.cloned.1.call-start = ((), (), s32[]{:S(2)}) async-start(), calls=%async_computation.4 | async-start | bytes 2228224 | tf_op jit(solution)/shard_map/reduce_scatter | solution.py:11
  9.2 86.8 %copy-start.6 = (f32[1,2048,128]{2,1,0:T(8,128)S(1)}, f32[1,2048,128]{2,1,0:T(8,128)}, u32[]{:S(2)}) copy-start(f32[1,2048,128]{2,1,0:T(8,128)} %param.21) | copy-start | bytes 3145732
  13.9 86.2 %copy-start.10 = (s32[16]{0:T(128)S(1)}, s32[16]{0:T(128)}, u32[]{:S(2)}) copy-start(s32[16]{0:T(128)} %param.30) | copy-start | bytes 196
  13.9 165.1 %reduce-scatter.7.cloned.1.call-start = ((), (), s32[]{:S(2)}) async-start(), calls=%async_computation.5 | async-start | bytes 2228224 | tf_op jit(solution)/shard_map/reduce_scatter | solution.py:11
  100.1 196.6 %all-reduce.8.cloned.1.call-start = ((), (), s32[]{:S(2)}) async-start(), calls=%async_computation.6 | async-start | bytes 4194304 | tf_op jit(solution)/shard_map/psum | solution.py:91
  181.8 220.7 %all-reduce.10.cloned.1.call-start = ((), (), s32[]{:S(2)}) async-start(), calls=%async_computation.7 | async-start | bytes 2097152 | tf_op jit(solution)/shard_map/psum | solution.py:22
  300.7 101.8 %copy-start.4 = (f32[4,256,256]{2,1,0:T(8,128)S(1)}, f32[4,256,256]{2,1,0:T(8,128)}, u32[]{:S(2)}) copy-start(f32[4,256,256]{2,1,0:T(8,128)} %param.25) | copy-start | bytes 3145732
  305.5 100.6 %copy-start.9 = (s32[4,32]{1,0:T(4,128)S(1)}, s32[4,32]{1,0:T(4,128)}, u32[]{:S(2)}) copy-start(s32[4,32]{1,0:T(4,128)} %param.33) | copy-start | bytes 1540
  305.5 211.6 %all-reduce.12.cloned.1.call-start = ((), (), s32[]{:S(2)}) async-start(), calls=%async_computation.8 | async-start | bytes 2097152 | tf_op jit(solution)/shard_map/psum | solution.py:26
  405.9 218.6 %all-reduce.14.cloned.1.call-start = ((), (), s32[]{:S(2)}) async-start(), calls=%async_computation.9 | async-start | bytes 1310720 | tf_op jit(solution)/shard_map/psum | solution.py:22
  522.5 2.4 copy-start.7
  525.1 99.4 %copy-start.3 = (f32[640,640]{1,0:T(8,128)S(1)}, f32[640,640]{1,0:T(8,128)}, u32[]{:S(2)}) copy-start(f32[640,640]{1,0:T(8,128)} %param.29) | copy-start | bytes 4915204
  529.2 209.5 %all-reduce.16.cloned.1.call-start = ((), (), s32[]{:S(2)}) async-start(), calls=%async_computation.10 | async-start | bytes 1310720 | tf_op jit(solution)/shard_map/psum | solution.py:26
  628.5 214.1 %all-reduce.18.cloned.1.call-start = ((), (), s32[]{:S(2)}) async-start(), calls=%async_computation.11 | async-start | bytes 2097152 | tf_op jit(solution)/shard_map/psum | solution.py:22
  740.1 5.4 copy-start.1
  745.5 212.4 %all-reduce.20.cloned.1.call-start = ((), (), s32[]{:S(2)}) async-start(), calls=%async_computation.12 | async-start | bytes 2097152 | tf_op jit(solution)/shard_map/psum | solution.py:26
  846.7 199.8 %reduce-scatter.9.cloned.1.call-start = ((), (), s32[]{:S(2)}) async-start(), calls=%async_computation.13 | async-start | bytes 2228224 | tf_op jit(solution)/shard_map/reduce_scatter | solution.py:11
  960.4 3.4 copy-start.5
  963.8 82.6 %copy-start.8 = (f32[128,256]{0,1:T(8,128)S(1)}, f32[128,256]{0,1:T(8,128)}, u32[]{:S(2)}) copy-start(f32[128,256]{0,1:T(8,128)} %reduce-scatter.5.cloned.1.call-done) | copy-start | bytes 393220
  967.1 83.8 %copy-start.2 = (f32[4,256,256]{1,2,0:T(8,128)S(1)}, f32[4,256,256]{1,2,0:T(8,128)}, u32[]{:S(2)}) copy-start(f32[4,256,256]{1,2,0:T(8,128)} %all-reduce.20.cloned.1.call-done) | copy-start | bytes 3145732
  967.1 162.7 %reduce-scatter.11.cloned.1.call-start = ((), (), s32[]{:S(2)}) async-start(), calls=%async_computation.14 | async-start | bytes 2228224 | tf_op jit(solution)/shard_map/reduce_scatter | solution.py:11
Sparse Core Ops, SparseCore 0:
  14.0 81.9 reduce-scatter.4
  100.2 78.7 reduce-scatter.6
  182.0 114.7 all-reduce.7
  305.6 96.8 all-reduce.9
  406.0 111.1 all-reduce.11
  529.3 95.0 all-reduce.13
  628.6 110.0 all-reduce.15
  745.6 97.0 all-reduce.17
  846.8 111.0 all-reduce.19
  967.2 79.1 reduce-scatter.8
  1051.0 78.7 reduce-scatter.10
where the time goes:
time: 1140 us
  waiting for transfers between devices  1050 us (92%)
  matrix products  47.5 us (4%)
  local copies, waits for them, and re-layouts  18.8 us (2%)
  between operations  14.1 us (1%)
    psum x3, waiting for transfers between devices, across_subtree(): return lax.psum(partial_value, 'subtree')  330 us
    reduce_scatter x4, waiting for transfers between devices, leaf_product(): lax.psum_scatter(jnp.dot(matrix, vector, preferred_element_type=jnp.float...  314 us
    psum x3, waiting for transfers between devices, across_front(): return lax.psum(partial_value, 'front')  289 us
    psum x1, waiting for transfers between devices, on_device(): assembled = lax.psum(placed, 'subtree')  115 us
  transfers between devices with their start and end apart: 11, of which 11 were waited for; matrix products, arithmetic and copies ran while one was open for 1% of the time, Pallas kernels for 0%

commit v1 on v0

v1 whole, which is shorter than its diff:
```python
import types

import jax
import jax.numpy as jnp
from jax import lax
from jax.experimental import pallas as pl
from jax.experimental.pallas import tpu as pltpu
from jax.sharding import PartitionSpec as P

MESH = pl.DeviceIdType.MESH
F32 = jnp.float32
BF16 = jnp.bfloat16
LANES = 128
FRONT_LEAF = ((0, 64), (1024, 64))
FRONT_MID = ((0, 32), (512, 32))
FRONT_ROOT = ((0, 24), (384, 16))

MATRICES = (
    (2048, 128),
    (2048, 128),
    (4, 256, 256),
    (4, 256, 256),
    (640, 640),
    (640, 640),
    (4, 256, 256),
    (4, 256, 256),
    (2048, 128),
    (2048, 128),
)
LEAF_LOWER, LEAF_BELOW, MID_LOWER, MID_BELOW, ROOT_LOWER = range(5)
ROOT_UPPER, MID_RIGHT, MID_UPPER, LEAF_RIGHT, LEAF_UPPER = range(5, 10)


def vmem(*shape):
    return pltpu.VMEM(shape, F32)


def front_scratch(layout):
    return [dict(r1=vmem(3, 4 * unit, LANES), r2=vmem(3, unit, LANES)) for _, unit in layout]


def exchange_scratch(layout):
    return [dict(r1=vmem(3, 4 * unit, LANES), r2=vmem(4, 4 * unit, LANES)) for _, unit in layout]


def subtree_scratch(blocks):
    return dict(core=vmem(8, blocks, 8, LANES), ring=vmem(7, blocks, 8, LANES))


def chain_scratch():
    return dict(
        part=vmem(2048, LANES),
        zpart8=vmem(16, 8, 8, LANES),
        zpart5=vmem(16, 5, 8, LANES),
        leaf_fwd=vmem(128, LANES),
        contrib=vmem(16, 8, LANES),
        children=vmem(16, 8, LANES),
        update=vmem(8, 8, LANES),
        pivot=vmem(16, 8, 8, LANES),
        mid_fwd=vmem(1024, LANES),
        start=vmem(16, 5, 8, LANES),
        root_fwd=vmem(640, LANES),
        root_sol=vmem(16, 5, 8, LANES),
        mid_back=vmem(1024, LANES),
        mid_sol=vmem(16, 8, 8, LANES),
        p1=front_scratch(FRONT_LEAF),
        p2=front_scratch(FRONT_LEAF),
        x4=exchange_scratch(FRONT_MID),
        z5=subtree_scratch(8),
        x6=exchange_scratch(FRONT_ROOT),
        z7=subtree_scratch(5),
        x8=exchange_scratch(FRONT_MID),
        z9=subtree_scratch(8),
        p10=front_scratch(FRONT_LEAF),
        p11=front_scratch(FRONT_LEAF),
        x=pltpu.VMEM((2048, 256), BF16),
    )


SCRATCH = dict(
    raw=[vmem(*shape) for shape in MATRICES],
    split=[pltpu.VMEM(shape[:-1] + (2 * shape[-1],), BF16) for shape in MATRICES],
    leaf_rhs=vmem(128, 256),
    mid_rhs=vmem(8, 8, 256),
    root_rhs=vmem(5, 8, 256),
    out_leaf=vmem(128, 256),
    out_mid=vmem(8, 16, 8, 256),
    out_root=vmem(5, 16, 8, 256),
    chains=[chain_scratch(), chain_scratch()],
)
SHAPES, TREE = jax.tree.flatten(SCRATCH)
SEMS = 512
ORDER = (0, 0, 1, 0, 1, 0, 1, 0, 0, 1, 0, 1, 0, 1, 0, 0, 1, 1, 0, 0, 1, 1, 0, 1, 0, 1, 0, 0, 1, 0, 1, 0, 1, 0, 1, 0, 1, 0, 1, 0, 1, 0, 1, 0, 1, 1, 0, 0, 1, 1, 0, 1, 1, 0, 0, 1, 0, 1, 1, 1, 0, 1, 0, 1, 1, 0)


def named(tree):
    if isinstance(tree, dict):
        return types.SimpleNamespace(**{key: named(value) for key, value in tree.items()})
    if isinstance(tree, list):
        return [named(value) for value in tree]
    return tree


def split(value):
    high = value.astype(BF16)
    low = (value - high.astype(F32)).astype(BF16)
    return high, low


def kernel(*refs):
    leaf_rhs_ref, mid_rhs_ref, root_rhs_ref = refs[:3]
    matrix_refs = refs[3:13]
    parent_ref, sizes_ref, leaf_map_ref, mid_map_ref = refs[13:17]
    out_leaf, out_mid, out_root = refs[17:20]
    scratch = named(jax.tree.unflatten(TREE, refs[20 : 20 + len(SHAPES)]))
    send_sems, recv_sems, load_sems, out_sems = refs[20 + len(SHAPES) :]

    s = lax.axis_index("subtree")
    f = lax.axis_index("front")
    xi, yi = f // 4, f % 4
    zi, ci = s // 2, s % 2
    rank = ci * 8 + zi

    def device(dx=0, dy=0, dz=0, dc=0):
        return (
            ((zi + dz) % 8) * 2 + (ci + dc) % 2,
            ((xi + dx) % 4) * 4 + (yi + dy) % 4,
        )

    def load(index, src, dst):
        copy = pltpu.make_async_copy(src, dst, load_sems.at[index])
        copy.start()
        return copy

    load_leaf_rhs = load(10, leaf_rhs_ref, scratch.leaf_rhs)
    loads = [load(0, matrix_refs[0], scratch.raw[0])]

    barrier = pltpu.get_barrier_semaphore()
    partners = [device(dx=d) for d in (1, 2, 3)] + [device(dy=d) for d in (1, 2, 3)]
    partners += [device(dz=d, dc=c) for d in range(8) for c in range(2) if (d, c) != (0, 0)]
    for partner in partners:
        pl.semaphore_signal(barrier, inc=1, device_id=partner, device_id_type=MESH)

    loads[0].wait()
    loads += [load(i, matrix_refs[i], scratch.raw[i]) for i in range(1, 10)]
    load_mid_rhs = load(11, mid_rhs_ref.at[:, rank], scratch.mid_rhs)
    load_root_rhs = load(12, root_rhs_ref.at[:, rank], scratch.root_rhs)

    def cast(name):
        if name != LEAF_LOWER:
            loads[name].wait()
        src, dst = scratch.raw[name], scratch.split[name]
        width = src.shape[-1]
        if len(src.shape) == 3:

            def body(i, carry):
                high, low = split(src[i])
                dst[i, :, 0:width] = high
                dst[i, :, width : 2 * width] = low
                return carry

            lax.fori_loop(0, src.shape[0], body, 0)
        else:
            tile = 256 if width == 128 else 64

            def body(i, carry):
                rows = pl.ds(pl.multiple_of(i * tile, tile), tile)
                high, low = split(src[rows, :])
                dst[rows, 0:width] = high
                dst[rows, width : 2 * width] = low
                return carry

            lax.fori_loop(0, src.shape[0] // tile, body, 0)

    counter = [0]
    first_send = [True]

    def chain(h):
        mine = scratch.chains[h]
        lanes = slice(h * LANES, (h + 1) * LANES)
        pending = []

        def send(src, dst, target):
            if first_send[0]:
                pl.semaphore_wait(barrier, len(partners))
                first_send[0] = False
            index = counter[0]
            counter[0] += 1
            copy = pltpu.make_async_remote_copy(
                src_ref=src,
                dst_ref=dst,
                send_sem=send_sems.at[index],
                recv_sem=recv_sems.at[index],
                device_id=target,
                device_id_type=MESH,
            )
            copy.start()
            pending.append(copy)
            return copy

        def flush():
            for copy in pending:
                copy.wait_send()
            pending.clear()

        def arrive(copies):
            for copy in copies:
                copy.wait_recv()

        def put_x(row, value):
            depth = value.shape[0]
            high, low = split(value)
            x = mine.x
            for r in (row, row + depth):
                x[r : r + depth, 0:LANES] = high
                x[r : r + depth, LANES : 2 * LANES] = low

        def dot(a, b):
            both = jnp.dot(a, b, preferred_element_type=F32)
            return both[:, :LANES] + both[:, LANES:]

        def position(half):
            return (xi, yi) if half == 0 else (yi, xi)

        def along(half, primary, d):
            use_x = (half == 0) == primary
            return device(dx=d) if use_x else device(dy=d)

        def front_scatter(bufs, layout):
            part = mine.part
            copies = []
            for half, (base, unit) in enumerate(layout):
                ia, ib = position(half)
                got = bufs[half].r1
                mineset = []
                for d in (2, 1, 3):
                    to = (ia + d) % 4
                    rows = pl.ds(pl.multiple_of(base + to * (4 * unit), 8), 4 * unit)
                    mineset.append(send(part.at[rows], got.at[d - 1], along(half, True, d)))
                copies.append(mineset)
            yield
            second = []
            for half, (base, unit) in enumerate(layout):
                ia, ib = position(half)
                got = bufs[half].r1
                arrive(copies[half])
                own = pl.multiple_of(base + ia * (4 * unit), 8)
                rows = pl.ds(own, 4 * unit)
                part[rows, :] = (part[rows, :] + got[0]) + (got[1] + got[2])
                got2 = bufs[half].r2
                mineset = []
                for d in (2, 1, 3):
                    to = (ib + d) % 4
                    rows = pl.ds(pl.multiple_of(own + to * unit, 8), unit)
                    mineset.append(send(part.at[rows], got2.at[d - 1], along(half, False, d)))
                second.append(mineset)
            yield
            sums = []
            for half, (base, unit) in enumerate(layout):
                ia, ib = position(half)
                got2 = bufs[half].r2
                arrive(second[half])
                rows = pl.ds(pl.multiple_of(base + ia * (4 * unit) + ib * unit, 8), unit)
                sums.append((part[rows, :] + got2[0]) + (got2[1] + got2[2]))
            return sums

        def front_reduce(bufs, layout, full, minuend=None):
            part = mine.part
            first = []
            for half, (base, unit) in enumerate(layout):
                ia, _ = position(half)
                copies = []
                for d in (2, 1, 3):
                    to = (ia + d) % 4
                    rows = pl.ds(pl.multiple_of(base + to * (4 * unit), 8), 4 * unit)
                    copies.append(send(part.at[rows], bufs[half].r1.at[d - 1], along(half, True, d)))
                first.append(copies)
            yield
            second = []
            for half, (base, unit) in enumerate(layout):
                ia, ib = position(half)
                got, got2 = bufs[half].r1, bufs[half].r2
                arrive(first[half])
                rows = pl.ds(pl.multiple_of(base + ia * (4 * unit), 8), 4 * unit)
                got2[ib] = (part[rows, :] + got[0]) + (got[1] + got[2])
                second.append(
                    [send(got2.at[ib], got2.at[ib], along(half, False, d)) for d in (2, 1, 3)]
                )
            yield
            last = []
            for half, (base, unit) in enumerate(layout):
                ia, _ = position(half)
                got2 = bufs[half].r2
                arrive(second[half])
                rows = pl.ds(pl.multiple_of(base + ia * (4 * unit), 8), 4 * unit)
                total = (got2[0] + got2[1]) + (got2[2] + got2[3])
                full[rows, :] = total if minuend is None else minuend[rows, :] - total
                last.append(
                    [send(full.at[rows], full.at[rows], along(half, True, d)) for d in (2, 1, 3)]
                )
            yield
            for copies in last:
                arrive(copies)

        def subtree_scatter(bufs, zpart):
            got = bufs.core
            theirs = pl.ds(pl.multiple_of((1 - ci) * 8, 8), 8)
            copy = send(zpart.at[theirs], got, device(dc=1))
            yield
            arrive([copy])
            start = pl.multiple_of(ci * 8, 8)
            zpart[pl.ds(start, 8)] = zpart[pl.ds(start, 8)] + got[...]
            ring = bufs.ring
            copies = []
            for d in (4, 3, 5, 2, 6, 1, 7):
                to = (zi + d) % 8
                copies.append(send(zpart.at[start + to], ring.at[d - 1], device(dz=d)))
            yield
            arrive(copies)
            a = (ring[0] + ring[1]) + (ring[2] + ring[3])
            b = (ring[4] + ring[5]) + (ring[6] + zpart[rank])
            return a + b

        def subtree_gather(full, chunk):
            full[rank] = chunk
            near = (1, 7, 2, 6, 3, 5, 4)
            copies = {d: send(full.at[rank], full.at[rank], device(dz=d)) for d in reversed(near)}
            across = [send(full.at[rank], full.at[rank], device(dc=1))]
            yield
            for d in near:
                arrive([copies[d]])
                slot = ci * 8 + (zi + 8 - d) % 8
                across.append(send(full.at[slot], full.at[slot], device(dc=1)))
            yield
            arrive(across)

        def leaf_product(name):
            flush()
            part, x, a = mine.part, mine.x, scratch.split[name]

            def body(j, carry):
                rows = pl.ds(pl.multiple_of(j * 256, 256), 256)
                y = dot(a[rows, :], x[0:256, :])
                for k in range(2):
                    block = 2 * j + k
                    low = pl.multiple_of(block * 64, 64)
                    high = pl.multiple_of(1024 + ((block % 4) * 4 + block // 4) * 64, 64)
                    part[pl.ds(low, 64), :] = y[k * 128 : k * 128 + 64]
                    part[pl.ds(high, 64), :] = y[k * 128 + 64 : k * 128 + 128]
                return carry

            lax.fori_loop(0, 8, body, 0)

        def mid_product(name, across_subtree):
            flush()
            x, a = mine.x, scratch.split[name]

            def body(p, carry):
                y = dot(a[p], x[pl.ds(pl.multiple_of(p * 512, 512), 512), :])
                if across_subtree:
                    y = y.reshape(2, 16, 8, LANES)
                    mine.zpart8[:, 2 * p] = y[0]
                    mine.zpart8[:, 2 * p + 1] = y[1]
                else:
                    mine.part[pl.ds(pl.multiple_of(p * 256, 256), 256), :] = y
                return carry

            lax.fori_loop(0, 4, body, 0)

        def root_product(name, across_subtree):
            flush()
            x, a = mine.x, scratch.split[name]

            def body(q, carry):
                rows = pl.ds(pl.multiple_of(q * 128, 128), 128)
                y = dot(a[rows, :], x[0:1280, :])
                if across_subtree:
                    mine.zpart5[:, q] = y.reshape(16, 8, LANES)
                else:
                    mine.part[rows, :] = y
                return carry

            lax.fori_loop(0, 5, body, 0)

        def block_of(full, t):
            return full[:, t].reshape(128, LANES)

        def root_slot(p, k):
            return jnp.clip(mid_map_ref[p, 2 * f + k] - 5 * f, 0, 4)

        positions = f * 128 + lax.broadcasted_iota(jnp.int32, (128, LANES), 0)
        live = (positions < sizes_ref[s]).astype(F32)
        lead = h == 0

        if lead:
            load_leaf_rhs.wait()
            cast(LEAF_LOWER)
        put_x(0, live * scratch.leaf_rhs[:, lanes])
        leaf_product(LEAF_LOWER)
        stage = front_scatter(mine.p1, FRONT_LEAF)
        next(stage)
        if lead:
            cast(LEAF_BELOW)
        yield
        sums = yield from stage
        leaf_fwd = live * jnp.concatenate(sums, axis=0)
        mine.leaf_fwd[...] = leaf_fwd

        put_x(0, leaf_fwd)
        leaf_product(LEAF_BELOW)
        stage = front_scatter(mine.p2, FRONT_LEAF)
        next(stage)
        if lead:
            cast(MID_LOWER)
        yield
        sums = yield from stage
        contrib = -jnp.concatenate(sums, axis=0)

        mine.contrib[...] = contrib.reshape(16, 8, LANES)
        children = mine.children
        children[s] = mine.contrib[rank]
        copies = []
        for d in (4, 3, 5, 2, 6, 1, 7, 0):
            for c in range(2):
                if (d, c) != (0, 0):
                    to = ((ci + c) % 2) * 8 + (zi + d) % 8
                    copies.append(send(mine.contrib.at[to], children.at[s], device(dz=d, dc=c)))
        if lead:
            cast(MID_BELOW)
            load_mid_rhs.wait()
        yield
        arrive(copies)
        placed = [jnp.zeros((8, LANES), F32) for _ in range(16)]
        for g in range(16):
            block = leaf_map_ref[g, f]
            upper = block >= 32
            slot = block - 2 * f - jnp.where(upper, 32, 0)
            target = parent_ref[g] * 4 + jnp.where(upper, 2, 0) + slot
            value = children[g]
            for t in range(16):
                placed[t] = placed[t] + jnp.where(target == t, value, 0.0)
        rhs = scratch.mid_rhs
        pivot = [rhs[t, :, lanes] + placed[(t // 2) * 4 + t % 2] for t in range(8)]
        mine.update[...] = jnp.stack([placed[(t // 2) * 4 + 2 + t % 2] for t in range(8)])
        yield from subtree_gather(mine.pivot, jnp.stack(pivot))

        for p in range(4):
            full = mine.pivot
            put_x(512 * p, jnp.concatenate([block_of(full, 2 * p), block_of(full, 2 * p + 1)], axis=0))
        mid_product(MID_LOWER, False)
        stage = front_reduce(mine.x4, FRONT_MID, mine.mid_fwd)
        next(stage)
        if lead:
            cast(ROOT_LOWER)
        yield
        yield from stage

        for p in range(4):
            put_x(512 * p, mine.mid_fwd[256 * p : 256 * p + 256, :])
        mid_product(MID_BELOW, True)
        stage = subtree_scatter(mine.z5, mine.zpart8)
        next(stage)
        yield
        next(stage)
        if lead:
            cast(ROOT_UPPER)
            load_root_rhs.wait()
        yield
        chunk = mine.update[...] - (yield from stage)
        start = [scratch.root_rhs[q, :, lanes] for q in range(5)]
        for p in range(4):
            for k in range(2):
                slot = mid_map_ref[p, 2 * f + k] - 5 * f
                for q in range(5):
                    start[q] = start[q] + jnp.where(slot == q, chunk[2 * p + k], 0.0)
        yield from subtree_gather(mine.start, jnp.stack(start))

        put_x(0, jnp.concatenate([block_of(mine.start, q) for q in range(5)], axis=0))
        root_product(ROOT_LOWER, False)
        stage = front_reduce(mine.x6, FRONT_ROOT, mine.root_fwd)
        next(stage)
        if lead:
            cast(MID_RIGHT)
        yield
        yield from stage

        put_x(0, mine.root_fwd[...])
        root_product(ROOT_UPPER, True)
        stage = subtree_scatter(mine.z7, mine.zpart5)
        next(stage)
        yield
        next(stage)
        if lead:
            cast(MID_UPPER)
        yield
        chunk = yield from stage
        yield from subtree_gather(mine.root_sol, chunk)

        for p in range(4):
            ext = [
                block_of(mine.root_sol, root_slot(p, k)) for k in range(2)
            ]
            put_x(512 * p, jnp.concatenate(ext, axis=0))
        mid_product(MID_RIGHT, False)
        stage = front_reduce(mine.x8, FRONT_MID, mine.mid_back, mine.mid_fwd)
        next(stage)
        if lead:
            cast(LEAF_RIGHT)
        for q in range(5):
            scratch.out_root[q, :, :, lanes] = mine.root_sol[:, q]
        yield
        yield from stage

        for p in range(4):
            put_x(512 * p, mine.mid_back[256 * p : 256 * p + 256, :])
        mid_product(MID_UPPER, True)
        stage = subtree_scatter(mine.z9, mine.zpart8)
        next(stage)
        yield
        next(stage)
        if lead:
            cast(LEAF_UPPER)
        yield
        chunk = yield from stage
        yield from subtree_gather(mine.mid_sol, chunk)

        block = leaf_map_ref[s, f]
        p = parent_ref[s]
        upper = block >= 32
        slot = jnp.clip(block - 2 * f - jnp.where(upper, 32, 0), 0, 1)
        from_sol = block_of(mine.mid_sol, 2 * p + slot)
        from_ext = block_of(mine.root_sol, root_slot(p, slot))
        put_x(0, jnp.where(upper, from_ext, from_sol))
        leaf_product(LEAF_RIGHT)
        stage = front_scatter(mine.p10, FRONT_LEAF)
        next(stage)
        for t in range(8):
            scratch.out_mid[t, :, :, lanes] = mine.mid_sol[:, t]
        yield
        sums = yield from stage
        put_x(0, live * (mine.leaf_fwd[...] - jnp.concatenate(sums, axis=0)))

        leaf_product(LEAF_UPPER)
        sums = yield from front_scatter(mine.p11, FRONT_LEAF)
        scratch.out_leaf[:, lanes] = live * jnp.concatenate(sums, axis=0)
        flush()

    chains = [chain(0), chain(1)]
    for which in ORDER:
        next(chains[which], None)

    outs = [
        pltpu.make_async_copy(scratch.out_leaf, out_leaf, out_sems.at[0]),
        pltpu.make_async_copy(scratch.out_mid, out_mid, out_sems.at[1]),
        pltpu.make_async_copy(scratch.out_root, out_root, out_sems.at[2]),
    ]
    for copy in outs:
        copy.start()
    for copy in outs:
        copy.wait()


def on_device(
    leaf_rhs,
    mid_rhs,
    root_rhs,
    leaf_lower,
    leaf_below,
    leaf_right,
    leaf_upper,
    mid_lower,
    mid_below,
    mid_right,
    mid_upper,
    root_lower,
    root_upper,
    leaf_parent,
    leaf_sizes,
    leaf_map,
    mid_map,
):
    operands = [leaf_rhs[0], mid_rhs.reshape(8, 16, 8, 256), root_rhs.reshape(5, 16, 8, 256)]
    operands += [leaf_lower[0], leaf_below[0], mid_lower, mid_below, root_lower]
    operands += [root_upper, mid_right, mid_upper, leaf_right[0], leaf_upper[0]]
    anywhere = pl.BlockSpec(memory_space=pl.ANY)
    scalars = pl.BlockSpec(memory_space=pltpu.SMEM)
    leaf_sol, mid_sol, root_sol = pl.pallas_call(
        kernel,
        out_shape=(
            jax.ShapeDtypeStruct((128, 256), F32),
            jax.ShapeDtypeStruct((8, 16, 8, 256), F32),
            jax.ShapeDtypeStruct((5, 16, 8, 256), F32),
        ),
        in_specs=[anywhere] * len(operands) + [scalars] * 4,
        out_specs=(anywhere,) * 3,
        scratch_shapes=SHAPES
        + [
            pltpu.SemaphoreType.DMA((SEMS,)),
            pltpu.SemaphoreType.DMA((SEMS,)),
            pltpu.SemaphoreType.DMA((13,)),
            pltpu.SemaphoreType.DMA((3,)),
        ],
        compiler_params=pltpu.CompilerParams(
            collective_id=0, has_side_effects=True, vmem_limit_bytes=60 * 2**20
        ),
        name="solve",
    )(*operands, leaf_parent, leaf_sizes, leaf_map, mid_map)
    return leaf_sol[None], mid_sol.reshape(4, 256, 256), root_sol.reshape(640, 256)


def solution(mesh):
    return jax.shard_map(
        on_device,
        mesh=mesh,
        in_specs=(
            P("subtree", "front", None),
            P(None, "front", None),
            P("front", None),
            P("subtree", None, "front"),
            P("subtree", None, "front"),
            P("subtree", None, "front"),
            P("subtree", None, "front"),
            P(None, "subtree", "front"),
            P(None, "front", "subtree"),
            P(None, "subtree", "front"),
            P(None, "front", "subtree"),
            P("subtree", "front"),
            P("front", "subtree"),
            P(),
            P(),
            P(),
            P(),
        ),
        out_specs=(P("subtree", "front", None), P(None, "front", None), P("front", None)),
        check_vma=False,
    )
```

time: 1140 us -> 215 us (0.19)
  waiting for transfers between devices: 1050 us -> 0 us
  Pallas kernels: 0 us -> 209 us
  matrix products: 47.5 us -> 0 us
  local copies, waits for them, and re-layouts: 18.8 us -> 4.76 us
  between operations: 14.1 us -> 0.66 us
    psum x7 -> x0, waiting for transfers between devices: 734 us -> none  [the longest x3 330 us: across_subtree(): return lax.psum(partial_value, 'subtree')]
    reduce_scatter x4 -> x0, waiting for transfers between devices: 314 us -> none  [leaf_product(): lax.psum_scatter(jnp.dot(matrix, vector, preferred_element_type=jnp.float...]
    pallas_call x0 -> x1, Pallas kernels: none -> 209 us  [on_device(): pl.pallas_call(kernel, out_shape=(jax.ShapeDtypeStruct((128, 256), F32),...]
    dot_general x13 -> x0, matrix products: 47.5 us -> none  [the longest x4 16.3 us: leaf_product(): jnp.dot(matrix, vector, preferred_element_type=jnp.float32, precision=lax...]
  transfers between devices with their start and end apart: 11 -> 0, of which waited for: 11 -> 0; matrix products, arithmetic and copies ran while one was open for 1% -> 0% of each run, Pallas kernels for 0% -> 0%
where the time goes in v1:
time: 215 us
  Pallas kernels  209 us (97%)
  local copies, waits for them, and re-layouts  4.76 us (2%)
    pallas_call x1, Pallas kernels, on_device(): pl.pallas_call(kernel, out_shape=(jax.ShapeDtypeStruct((128, 256), F32),...  209 us
    unnamed x5, local copies, waits for them, and re-layouts  4.76 us

profile of v1, /device:TPU:2, one launch (start us, length us, event | category | flops | bytes accessed | tf_op | source)
XLA Modules:
  0.0 214.7 jit_solution(2805818894224989733)
XLA Ops:
  0.6 209.3 %solve.1 = (f32[128,256]{1,0:T(8,128)}, f32[8,16,8,256]{3,2,1,0:T(8,128)}, f32[5,16,8,256]{3,2,1,0:T(8,128)}) custom-call(f32[128,256]{1,0:T(8,128)} %bitcast.19, f32[8,16,8,256]{3,2,1,0:T(8,128)} %bitcast.11, f32[5,16,8,256]{3,2,1,0:T(8,128)} %bitcast.17, f32[2048,128]{1,0:T(8,128)} %bitcast.12, f32[2048,128]{1,0:T(8,128)} %bitcast.13, ...), custom_call_target="tpu_custom_call" | custom-call | tf_op jit(solution)/shard_map/solve/pallas_call | solution.py:587
  209.9 0.0 copy-start
  209.9 1.6 copy.23
  211.6 2.3 %copy.24 = f32[4,256,256]{2,1,0:T(8,128)} copy(f32[4,256,256]{2,1,0:T(8,128)} %bitcast.10) | data formatting | bytes 2097152
  213.9 0.0 copy-done
  213.9 0.8 copy.25
Async XLA Ops:
  209.9 3.9 %copy-start = (f32[5,16,8,256]{3,2,1,0:T(8,128)S(1)}, f32[5,16,8,256]{3,2,1,0:T(8,128)}, u32[]{:S(2)}) copy-start(f32[5,16,8,256]{3,2,1,0:T(8,128)} %get-tuple-element.8) | copy-start | bytes 1966084

commit v2 on v1

--- a/solution.py
+++ b/solution.py
@@ -36,7 +36,7 @@
 
 
 def front_scratch(layout):
-    return [dict(r1=vmem(3, 4 * unit, LANES), r2=vmem(3, unit, LANES)) for _, unit in layout]
+    return [dict(relay=vmem(2, 2 * unit, LANES), r1=vmem(2, 4 * unit, LANES), r2=vmem(3, unit, LANES)) for _, unit in layout]
 
 
 def exchange_scratch(layout):
@@ -63,6 +63,9 @@
         root_sol=vmem(16, 5, 8, LANES),
         mid_back=vmem(1024, LANES),
         mid_sol=vmem(16, 8, 8, LANES),
+        mid_own=vmem(8, 8, LANES),
+        picked=vmem(16, 8, LANES),
+        leaf_ext=vmem(16, 8, LANES),
         p1=front_scratch(FRONT_LEAF),
         p2=front_scratch(FRONT_LEAF),
         x4=exchange_scratch(FRONT_MID),
@@ -89,8 +92,8 @@
     chains=[chain_scratch(), chain_scratch()],
 )
 SHAPES, TREE = jax.tree.flatten(SCRATCH)
-SEMS = 512
-ORDER = (0, 0, 1, 0, 1, 0, 1, 0, 0, 1, 0, 1, 0, 1, 0, 0, 1, 1, 0, 0, 1, 1, 0, 1, 0, 1, 0, 0, 1, 0, 1, 0, 1, 0, 1, 0, 1, 0, 1, 0, 1, 0, 1, 0, 1, 1, 0, 0, 1, 1, 0, 1, 1, 0, 0, 1, 0, 1, 1, 1, 0, 1, 0, 1, 1, 0)
+SEMS = 576
+ORDER = (0, 0, 1, 0, 1, 0, 1, 0, 0, 1, 0, 1, 0, 1, 0, 1, 0, 1, 0, 0, 1, 1, 0, 0, 1, 1, 0, 1, 0, 1, 0, 0, 1, 0, 1, 0, 1, 0, 1, 0, 1, 0, 1, 0, 1, 0, 1, 0, 1, 1, 0, 0, 1, 1, 0, 1, 0, 1, 0, 1, 0, 1, 1, 0, 1, 0, 1, 0, 1, 1, 0, 1)
 
 
 def named(tree):
@@ -133,7 +136,11 @@
         return copy
 
     load_leaf_rhs = load(10, leaf_rhs_ref, scratch.leaf_rhs)
-    loads = [load(0, matrix_refs[0], scratch.raw[0])]
+    quarters = [pl.ds(512 * i, 512) for i in range(4)]
+    firsts = [
+        load(13 + i, matrix_refs[0].at[rows], scratch.raw[0].at[rows])
+        for i, rows in enumerate(quarters)
+    ]
 
     barrier = pltpu.get_barrier_semaphore()
     partners = [device(dx=d) for d in (1, 2, 3)] + [device(dy=d) for d in (1, 2, 3)]
@@ -141,8 +148,9 @@
     for partner in partners:
         pl.semaphore_signal(barrier, inc=1, device_id=partner, device_id_type=MESH)
 
-    loads[0].wait()
-    loads += [load(i, matrix_refs[i], scratch.raw[i]) for i in range(1, 10)]
+    for copy in firsts:
+        copy.wait()
+    loads = [None] + [load(i, matrix_refs[i], scratch.raw[i]) for i in range(1, 10)]
     load_mid_rhs = load(11, mid_rhs_ref.at[:, rank], scratch.mid_rhs)
     load_root_rhs = load(12, root_rhs_ref.at[:, rank], scratch.root_rhs)
 
@@ -172,6 +180,13 @@
 
             lax.fori_loop(0, src.shape[0] // tile, body, 0)
 
+    outputs, ready = [], []
+
+    def output(index, src, dst):
+        copy = pltpu.make_async_copy(src, dst, out_sems.at[index])
+        copy.start()
+        outputs.append(copy)
+
     counter = [0]
     first_send = [True]
 
@@ -180,7 +195,9 @@
         lanes = slice(h * LANES, (h + 1) * LANES)
         pending = []
 
-        def send(src, dst, target):
+        late = []
+
+        def send(src, dst, target, kept=True):
             if first_send[0]:
                 pl.semaphore_wait(barrier, len(partners))
                 first_send[0] = False
@@ -195,13 +212,18 @@
                 device_id_type=MESH,
             )
             copy.start()
-            pending.append(copy)
+            (late if kept else pending).append(copy)
             return copy
 
         def flush():
             for copy in pending:
                 copy.wait_send()
             pending.clear()
+
+        def flush_late():
+            for copy in late:
+                copy.wait_send()
+            late.clear()
 
         def arrive(copies):
             for copy in copies:
@@ -228,31 +250,58 @@
 
         def front_scatter(bufs, layout):
             part = mine.part
-            copies = []
+
+            def rows_of(half, to, upper):
+                base, unit = layout[half]
+                return pl.ds(pl.multiple_of(base + to * (4 * unit) + 2 * unit * upper, 8), 2 * unit)
+
+            relayed, straight, summed = [], [], []
             for half, (base, unit) in enumerate(layout):
-                ia, ib = position(half)
-                got = bufs[half].r1
-                mineset = []
-                for d in (2, 1, 3):
-                    to = (ia + d) % 4
-                    rows = pl.ds(pl.multiple_of(base + to * (4 * unit), 8), 4 * unit)
-                    mineset.append(send(part.at[rows], got.at[d - 1], along(half, True, d)))
-                copies.append(mineset)
+                ia, _ = position(half)
+                copies = []
+                for side, d in ((0, 1), (1, 3)):
+                    rows = rows_of(half, (ia + 2) % 4, side)
+                    copies.append(send(part.at[rows], bufs[half].relay.at[side], along(half, True, d), False))
+                relayed.append(copies)
+            for half, (base, unit) in enumerate(layout):
+                ia, _ = position(half)
+                copies = []
+                for side, d in ((0, 1), (1, 3)):
+                    rows = rows_of(half, (ia + d) % 4, 1 - side)
+                    there = pl.ds(2 * unit * (1 - side), 2 * unit)
+                    copies.append(
+                        send(part.at[rows], bufs[half].r1.at[side, there], along(half, True, d), False)
+                    )
+                straight.append(copies)
+            yield
+            for half, (base, unit) in enumerate(layout):
+                ia, _ = position(half)
+                copies = []
+                for side, d in ((0, 1), (1, 3)):
+                    arrive([relayed[half][side]])
+                    rows = rows_of(half, (ia + d) % 4, side)
+                    part[rows, :] = part[rows, :] + bufs[half].relay[side]
+                    there = pl.ds(2 * unit * side, 2 * unit)
+                    copies.append(
+                        send(part.at[rows], bufs[half].r1.at[side, there], along(half, True, d), False)
+                    )
+                summed.append(copies)
             yield
             second = []
             for half, (base, unit) in enumerate(layout):
                 ia, ib = position(half)
                 got = bufs[half].r1
-                arrive(copies[half])
+                arrive(straight[half])
+                arrive(summed[half])
                 own = pl.multiple_of(base + ia * (4 * unit), 8)
                 rows = pl.ds(own, 4 * unit)
-                part[rows, :] = (part[rows, :] + got[0]) + (got[1] + got[2])
+                part[rows, :] = part[rows, :] + (got[0] + got[1])
                 got2 = bufs[half].r2
                 mineset = []
                 for d in (2, 1, 3):
                     to = (ib + d) % 4
                     rows = pl.ds(pl.multiple_of(own + to * unit, 8), unit)
-                    mineset.append(send(part.at[rows], got2.at[d - 1], along(half, False, d)))
+                    mineset.append(send(part.at[rows], got2.at[d - 1], along(half, False, d), False))
                 second.append(mineset)
             yield
             sums = []
@@ -273,7 +322,7 @@
                 for d in (2, 1, 3):
                     to = (ia + d) % 4
                     rows = pl.ds(pl.multiple_of(base + to * (4 * unit), 8), 4 * unit)
-                    copies.append(send(part.at[rows], bufs[half].r1.at[d - 1], along(half, True, d)))
+                    copies.append(send(part.at[rows], bufs[half].r1.at[d - 1], along(half, True, d), False))
                 first.append(copies)
             yield
             second = []
@@ -305,7 +354,7 @@
         def subtree_scatter(bufs, zpart):
             got = bufs.core
             theirs = pl.ds(pl.multiple_of((1 - ci) * 8, 8), 8)
-            copy = send(zpart.at[theirs], got, device(dc=1))
+            copy = send(zpart.at[theirs], got, device(dc=1), False)
             yield
             arrive([copy])
             start = pl.multiple_of(ci * 8, 8)
@@ -314,7 +363,7 @@
             copies = []
             for d in (4, 3, 5, 2, 6, 1, 7):
                 to = (zi + d) % 8
-                copies.append(send(zpart.at[start + to], ring.at[d - 1], device(dz=d)))
+                copies.append(send(zpart.at[start + to], ring.at[d - 1], device(dz=d), False))
             yield
             arrive(copies)
             a = (ring[0] + ring[1]) + (ring[2] + ring[3])
@@ -336,51 +385,33 @@
 
         def leaf_product(name):
             flush()
-            part, x, a = mine.part, mine.x, scratch.split[name]
-
-            def body(j, carry):
-                rows = pl.ds(pl.multiple_of(j * 256, 256), 256)
-                y = dot(a[rows, :], x[0:256, :])
-                for k in range(2):
-                    block = 2 * j + k
-                    low = pl.multiple_of(block * 64, 64)
-                    high = pl.multiple_of(1024 + ((block % 4) * 4 + block // 4) * 64, 64)
-                    part[pl.ds(low, 64), :] = y[k * 128 : k * 128 + 64]
-                    part[pl.ds(high, 64), :] = y[k * 128 + 64 : k * 128 + 128]
-                return carry
-
-            lax.fori_loop(0, 8, body, 0)
+            part = mine.part
+            y = dot(scratch.split[name][...], mine.x[0:256, :])
+            for block in range(16):
+                low, high = block * 64, 1024 + ((block % 4) * 4 + block // 4) * 64
+                part[low : low + 64, :] = y[block * 128 : block * 128 + 64]
+                part[high : high + 64, :] = y[block * 128 + 64 : block * 128 + 128]
 
         def mid_product(name, across_subtree):
             flush()
             x, a = mine.x, scratch.split[name]
-
-            def body(p, carry):
-                y = dot(a[p], x[pl.ds(pl.multiple_of(p * 512, 512), 512), :])
+            for p in range(4):
+                y = dot(a[p], x[512 * p : 512 * p + 512, :])
                 if across_subtree:
                     y = y.reshape(2, 16, 8, LANES)
                     mine.zpart8[:, 2 * p] = y[0]
                     mine.zpart8[:, 2 * p + 1] = y[1]
                 else:
-                    mine.part[pl.ds(pl.multiple_of(p * 256, 256), 256), :] = y
-                return carry
-
-            lax.fori_loop(0, 4, body, 0)
+                    mine.part[256 * p : 256 * p + 256, :] = y
 
         def root_product(name, across_subtree):
             flush()
-            x, a = mine.x, scratch.split[name]
-
-            def body(q, carry):
-                rows = pl.ds(pl.multiple_of(q * 128, 128), 128)
-                y = dot(a[rows, :], x[0:1280, :])
-                if across_subtree:
-                    mine.zpart5[:, q] = y.reshape(16, 8, LANES)
-                else:
-                    mine.part[rows, :] = y
-                return carry
-
-            lax.fori_loop(0, 5, body, 0)
+            y = dot(scratch.split[name][...], mine.x[0:1280, :])
+            if across_subtree:
+                for q in range(5):
+                    mine.zpart5[:, q] = y[128 * q : 128 * q + 128].reshape(16, 8, LANES)
+            else:
+                mine.part[0:640, :] = y
 
         def block_of(full, t):
             return full[:, t].reshape(128, LANES)
@@ -508,6 +539,9 @@
             cast(LEAF_RIGHT)
         for q in range(5):
             scratch.out_root[q, :, :, lanes] = mine.root_sol[:, q]
+        ready.append(8)
+        if ready.count(8) == 2:
+            output(2, scratch.out_root, out_root)
         yield
         yield from stage
 
@@ -521,42 +555,79 @@
         if lead:
             cast(LEAF_UPPER)
         yield
-        chunk = yield from stage
-        yield from subtree_gather(mine.mid_sol, chunk)
-
-        block = leaf_map_ref[s, f]
-        p = parent_ref[s]
-        upper = block >= 32
-        slot = jnp.clip(block - 2 * f - jnp.where(upper, 32, 0), 0, 1)
-        from_sol = block_of(mine.mid_sol, 2 * p + slot)
+        mine.mid_own[...] = yield from stage
+
+        def leaf_target(g):
+            block = leaf_map_ref[g, f]
+            upper = block >= 32
+            return parent_ref[g], jnp.clip(block - 2 * f - jnp.where(upper, 32, 0), 0, 1), upper
+
+        for g in range(16):
+            p, slot, _ = leaf_target(g)
+            mine.picked[g] = mine.mid_own[2 * p + slot]
+        mine.leaf_ext[rank] = mine.picked[s]
+        copies = []
+        for d in (4, 3, 5, 2, 6, 1, 7, 0):
+            for c in range(2):
+                if (d, c) != (0, 0):
+                    to = ((zi + d) % 8) * 2 + (ci + c) % 2
+                    copies.append(
+                        send(mine.picked.at[to], mine.leaf_ext.at[rank], device(dz=d, dc=c))
+                    )
+        gather = subtree_gather(mine.mid_sol, mine.mid_own[...])
+        next(gather)
+        yield
+        arrive(copies)
+
+        p, slot, upper = leaf_target(s)
+        from_sol = mine.leaf_ext[...].reshape(128, LANES)
         from_ext = block_of(mine.root_sol, root_slot(p, slot))
         put_x(0, jnp.where(upper, from_ext, from_sol))
         leaf_product(LEAF_RIGHT)
         stage = front_scatter(mine.p10, FRONT_LEAF)
         next(stage)
+        yield
+        next(stage)
+        next(gather)
+        yield
+        sums = yield from stage
+        put_x(0, live * (mine.leaf_fwd[...] - jnp.concatenate(sums, axis=0)))
+
+        leaf_product(LEAF_UPPER)
+        stage = front_scatter(mine.p11, FRONT_LEAF)
+        next(stage)
+        next(gather, None)
         for t in range(8):
             scratch.out_mid[t, :, :, lanes] = mine.mid_sol[:, t]
+        ready.append(10)
+        if ready.count(10) == 2:
+            output(1, scratch.out_mid, out_mid)
+        flush_late()
         yield
         sums = yield from stage
-        put_x(0, live * (mine.leaf_fwd[...] - jnp.concatenate(sums, axis=0)))
-
-        leaf_product(LEAF_UPPER)
-        sums = yield from front_scatter(mine.p11, FRONT_LEAF)
         scratch.out_leaf[:, lanes] = live * jnp.concatenate(sums, axis=0)
         flush()
+        flush_late()
 
     chains = [chain(0), chain(1)]
     for which in ORDER:
         next(chains[which], None)
 
-    outs = [
-        pltpu.make_async_copy(scratch.out_leaf, out_leaf, out_sems.at[0]),
-        pltpu.make_async_copy(scratch.out_mid, out_mid, out_sems.at[1]),
-        pltpu.make_async_copy(scratch.out_root, out_root, out_sems.at[2]),
-    ]
-    for copy in outs:
+    output(0, scratch.out_leaf, out_leaf)
+    for copy in outputs:
+        copy.wait()
+
+
+def copy_kernel(a, b, c, a_out, b_out, c_out, a_held, b_held, c_held, sems):
+    steps = ((b, b_held, b_out), (c, c_held, c_out), (a, a_held, a_out))
+    reads = [pltpu.make_async_copy(x, y, sems.at[i]) for i, (x, y, _) in enumerate(steps)]
+    writes = [pltpu.make_async_copy(y, z, sems.at[3 + i]) for i, (_, y, z) in enumerate(steps)]
+    for copy in reads:
         copy.start()
-    for copy in outs:
+    for read, write in zip(reads, writes):
+        read.wait()
+        write.start()
+    for copy in writes:
         copy.wait()
 
 
@@ -584,20 +655,21 @@
     operands += [root_upper, mid_right, mid_upper, leaf_right[0], leaf_upper[0]]
     anywhere = pl.BlockSpec(memory_space=pl.ANY)
     scalars = pl.BlockSpec(memory_space=pltpu.SMEM)
-    leaf_sol, mid_sol, root_sol = pl.pallas_call(
+    shapes = (
+        jax.ShapeDtypeStruct((128, 256), F32),
+        jax.ShapeDtypeStruct((8, 16, 8, 256), F32),
+        jax.ShapeDtypeStruct((5, 16, 8, 256), F32),
+    )
+    results = pl.pallas_call(
         kernel,
-        out_shape=(
-            jax.ShapeDtypeStruct((128, 256), F32),
-            jax.ShapeDtypeStruct((8, 16, 8, 256), F32),
-            jax.ShapeDtypeStruct((5, 16, 8, 256), F32),
-        ),
+        out_shape=shapes,
         in_specs=[anywhere] * len(operands) + [scalars] * 4,
         out_specs=(anywhere,) * 3,
         scratch_shapes=SHAPES
         + [
             pltpu.SemaphoreType.DMA((SEMS,)),
             pltpu.SemaphoreType.DMA((SEMS,)),
-            pltpu.SemaphoreType.DMA((13,)),
+            pltpu.SemaphoreType.DMA((17,)),
             pltpu.SemaphoreType.DMA((3,)),
         ],
         compiler_params=pltpu.CompilerParams(
@@ -605,6 +677,14 @@
         ),
         name="solve",
     )(*operands, leaf_parent, leaf_sizes, leaf_map, mid_map)
+    leaf_sol, mid_sol, root_sol = pl.pallas_call(
+        copy_kernel,
+        out_shape=shapes,
+        in_specs=[anywhere] * 3,
+        out_specs=(anywhere,) * 3,
+        scratch_shapes=[pltpu.VMEM(shape.shape, F32) for shape in shapes]
+        + [pltpu.SemaphoreType.DMA((6,))],
+    )(*results)
     return leaf_sol[None], mid_sol.reshape(4, 256, 256), root_sol.reshape(640, 256)
 
 

time: 215 us -> 203 us (0.944)
  Pallas kernels: 209 us -> 202 us
  local copies, waits for them, and re-layouts: 4.76 us -> 0 us
    pallas_call x1 -> x2, Pallas kernels: 209 us -> 202 us  [the longest x1 199 us: on_device(): pl.pallas_call(kernel, out_shape=shapes, in_specs=[anywhere] * len(operan...]
    unnamed x5 -> x0, local copies, waits for them, and re-layouts: 4.76 us -> none
where the time goes in v2:
time: 203 us; the launch traced here: 202 us
  Pallas kernels  202 us (100%)
    pallas_call x1, Pallas kernels, on_device(): pl.pallas_call(kernel, out_shape=shapes, in_specs=[anywhere] * len(operan...  199 us

profile of v2, /device:TPU:2, one launch (start us, length us, event | category | flops | bytes accessed | tf_op | source)
XLA Modules:
  0.0 202.3 jit_solution(8141108076859219086)
XLA Ops:
  0.6 199.0 %solve.1 = (f32[128,256]{1,0:T(8,128)}, f32[8,16,8,256]{3,2,1,0:T(8,128)}, f32[5,16,8,256]{3,2,1,0:T(8,128)}) custom-call(f32[128,256]{1,0:T(8,128)} %bitcast.16, f32[8,16,8,256]{3,2,1,0:T(8,128)} %bitcast.10, f32[5,16,8,256]{3,2,1,0:T(8,128)} %bitcast.15, f32[2048,128]{1,0:T(8,128)} %bitcast.11, f32[2048,128]{1,0:T(8,128)} %bitcast.12, ...), custom_call_target="tpu_custom_call" | custom-call | tf_op jit(solution)/shard_map/solve/pallas_call | solution.py:663
  199.7 2.5 %shard_map.184 = (f32[128,256]{1,0:T(8,128)}, f32[8,16,8,256]{3,2,1,0:T(8,128)}, f32[5,16,8,256]{3,2,1,0:T(8,128)}) custom-call(f32[128,256]{1,0:T(8,128)} %get-tuple-element.9.a, f32[8,16,8,256]{3,2,1,0:T(8,128)} %get-tuple-element.10.b, f32[5,16,8,256]{3,2,1,0:T(8,128)} %get-tuple-element.11.c), custom_call_target="tpu_custom_call" | custom-call | tf_op jit(solution)/shard_map/pallas_call | solution.py:680

commit v3 on v2

--- a/solution.py
+++ b/solution.py
@@ -93,7 +93,7 @@
 )
 SHAPES, TREE = jax.tree.flatten(SCRATCH)
 SEMS = 576
-ORDER = (0, 0, 1, 0, 1, 0, 1, 0, 0, 1, 0, 1, 0, 1, 0, 1, 0, 1, 0, 0, 1, 1, 0, 0, 1, 1, 0, 1, 0, 1, 0, 0, 1, 0, 1, 0, 1, 0, 1, 0, 1, 0, 1, 0, 1, 0, 1, 0, 1, 1, 0, 0, 1, 1, 0, 1, 0, 1, 0, 1, 0, 1, 1, 0, 1, 0, 1, 0, 1, 1, 0, 1)
+ORDER = (0, 0, 1, 0, 0, 1, 0, 1, 0, 1, 0, 1, 0, 1, 0, 1, 0, 1, 0, 0, 1, 1, 0, 0, 1, 1, 0, 1, 0, 1, 0, 0, 1, 0, 1, 0, 1, 0, 1, 0, 1, 0, 1, 0, 1, 0, 1, 0, 1, 1, 0, 0, 1, 1, 0, 1, 0, 1, 1, 0, 0, 1, 1, 0, 1, 0, 1, 0, 1, 1, 0, 1)
 
 
 def named(tree):
@@ -148,11 +148,12 @@
     for partner in partners:
         pl.semaphore_signal(barrier, inc=1, device_id=partner, device_id_type=MESH)
 
-    for copy in firsts:
-        copy.wait()
-    loads = [None] + [load(i, matrix_refs[i], scratch.raw[i]) for i in range(1, 10)]
-    load_mid_rhs = load(11, mid_rhs_ref.at[:, rank], scratch.mid_rhs)
-    load_root_rhs = load(12, root_rhs_ref.at[:, rank], scratch.root_rhs)
+    loads = []
+
+    def load_rest():
+        loads.extend([None] + [load(i, matrix_refs[i], scratch.raw[i]) for i in range(1, 10)])
+        loads.append(load(11, mid_rhs_ref.at[:, rank], scratch.mid_rhs))
+        loads.append(load(12, root_rhs_ref.at[:, rank], scratch.root_rhs))
 
     def cast(name):
         if name != LEAF_LOWER:
@@ -425,12 +426,15 @@
 
         if lead:
             load_leaf_rhs.wait()
+            for copy in firsts:
+                copy.wait()
             cast(LEAF_LOWER)
         put_x(0, live * scratch.leaf_rhs[:, lanes])
         leaf_product(LEAF_LOWER)
         stage = front_scatter(mine.p1, FRONT_LEAF)
         next(stage)
         if lead:
+            load_rest()
             cast(LEAF_BELOW)
         yield
         sums = yield from stage
@@ -458,7 +462,7 @@
                     copies.append(send(mine.contrib.at[to], children.at[s], device(dz=d, dc=c)))
         if lead:
             cast(MID_BELOW)
-            load_mid_rhs.wait()
+            loads[10].wait()
         yield
         arrive(copies)
         placed = [jnp.zeros((8, LANES), F32) for _ in range(16)]
@@ -495,7 +499,7 @@
         next(stage)
         if lead:
             cast(ROOT_UPPER)
-            load_root_rhs.wait()
+            loads[11].wait()
         yield
         chunk = mine.update[...] - (yield from stage)
         start = [scratch.root_rhs[q, :, lanes] for q in range(5)]

time: 203 us -> 201 us (level)
  no operation moved by 1% of the time
where the time goes in v3:
time: 201 us
  Pallas kernels  200 us (100%)
    pallas_call x1, Pallas kernels, on_device(): pl.pallas_call(kernel, out_shape=shapes, in_specs=[anywhere] * len(operan...  198 us

profile of v3, /device:TPU:2, one launch (start us, length us, event | category | flops | bytes accessed | tf_op | source)
XLA Modules:
  0.0 201.2 jit_solution(16777746468222438744)
XLA Ops:
  0.6 197.9 %solve.1 = (f32[128,256]{1,0:T(8,128)}, f32[8,16,8,256]{3,2,1,0:T(8,128)}, f32[5,16,8,256]{3,2,1,0:T(8,128)}) custom-call(f32[128,256]{1,0:T(8,128)} %bitcast.16, f32[8,16,8,256]{3,2,1,0:T(8,128)} %bitcast.10, f32[5,16,8,256]{3,2,1,0:T(8,128)} %bitcast.15, f32[2048,128]{1,0:T(8,128)} %bitcast.11, f32[2048,128]{1,0:T(8,128)} %bitcast.12, ...), custom_call_target="tpu_custom_call" | custom-call | tf_op jit(solution)/shard_map/solve/pallas_call | solution.py:667
  198.5 2.5 %shard_map.184 = (f32[128,256]{1,0:T(8,128)}, f32[8,16,8,256]{3,2,1,0:T(8,128)}, f32[5,16,8,256]{3,2,1,0:T(8,128)}) custom-call(f32[128,256]{1,0:T(8,128)} %get-tuple-element.9.a, f32[8,16,8,256]{3,2,1,0:T(8,128)} %get-tuple-element.10.b, f32[5,16,8,256]{3,2,1,0:T(8,128)} %get-tuple-element.11.c), custom_call_target="tpu_custom_call" | custom-call | tf_op jit(solution)/shard_map/pallas_call | solution.py:684
